TPU v7x, 128 devices: a whole 4x4x4 slice. The times are simulated.
128 devices in a mesh: grp: 8 (over x, core), mem: 16 (over z, y).
Axes of the slice: x: 4, y: 4, z: 4, core: 2. Of those that a mesh axis runs over, the one named last changes fastest.
Arguments:
- embeddings: bfloat16 [65536, 768], P(('grp', 'mem')), may hold values from -6 to 6
- initial_centroids: bfloat16 [104, 100, 768], P('grp'), may hold values from -6 to 6
- row_owner: int32 [65536, 1], P(('grp', 'mem')), may hold values from 0 to 127; in each aligned block of 512 rows (0 to 511, 512 to 1023, ...) at most 12 rows name the same one
- prefix_offset: int32 [65536], P(('grp', 'mem')), may hold values from 0 to 12
- first_assign: int32 [65536], P(('grp', 'mem')), may hold values from 0 to 99
- second_assign: int32 [65536], P(('grp', 'mem')), may hold values from 0 to 99
Outputs:
- distances: float32 [100, 65536], P(None, ('grp', 'mem'))
- first_distance: float32 [65536], P(('grp', 'mem'))
Inputs may be any that keep to these rules, and one draw needn't show every extreme that they name: `row_owner`: owners are numbered grp index times 16 plus mem index. At most 12 passages of one device have the same owner, and in every draw some owner has exactly 12 passages of some device.
All inputs are finite; a program needn't handle non-finite values.
Results may differ from a plain program's by a relative error of at most 0.00035.
Values may be sent and summed in bfloat16 or wider, within the bound.
No kernel may reach another device: no remote copies, remote signals or barrier semaphores. Data moves between devices by JAX's collectives and lax.ppermute only.
A program may use at most 128 MiB of HBM per device.

v0:
```python
import jax
import jax.numpy as jnp
from jax import lax
from jax.sharding import PartitionSpec as P

PRIOR = 16


def pick_block(total):
    for candidate in range(1024, 0, -1):
        if total % candidate == 0:
            return candidate
    return total


def body(embeddings, initial_centroids, row_owner, prefix_offset, first_assign, second_assign):
    row_count, feat_width = embeddings.shape
    group_codes = initial_centroids.shape[0]
    codes_two = initial_centroids.shape[1]
    clusters = group_codes * codes_two
    group_count = lax.axis_size("grp")
    member_count = lax.axis_size("mem")
    devices_all = group_count * member_count
    capacity = 2 * row_count // devices_all + 4
    slot_total = devices_all * capacity
    target = row_owner[:, 0]
    dest_table = (target[:, None] == jnp.arange(devices_all, dtype=jnp.int32)[None, :]).astype(
        jnp.int32
    )
    slot_rank = jnp.sum(jnp.cumsum(dest_table, axis=0) * dest_table, axis=1) - 1
    slot_index = target * capacity + slot_rank
    send_rows = jnp.zeros((slot_total, feat_width), jnp.bfloat16).at[slot_index].set(embeddings)
    labels = jnp.stack([prefix_offset, first_assign, second_assign], axis=1)
    send_labels = jnp.full((slot_total, 3), -1, jnp.int32).at[slot_index].set(labels)
    got_rows, got_labels = (
        lax.all_to_all(send_rows, ("grp", "mem"), split_axis=0, concat_axis=0, tiled=True),
        lax.all_to_all(send_labels, ("grp", "mem"), split_axis=0, concat_axis=0, tiled=True),
    )
    offsets = got_labels[:, 0]
    live = offsets >= 0
    ids_one = jnp.where(live, offsets * codes_two + got_labels[:, 1], -1)
    ids_two = jnp.where(live, offsets * codes_two + got_labels[:, 2], -1)
    squares = jnp.sum(jnp.square(got_rows.astype(jnp.float32)), axis=1)
    block_rows = pick_block(slot_total)
    block_count = slot_total // block_rows
    row_blocks = got_rows.reshape(block_count, block_rows, feat_width)
    cluster_range = jnp.arange(clusters, dtype=jnp.int32)

    def local_totals(cluster_ids):

        def add_block(carry, pieces):
            totals, counts = carry
            block_x, block_ids = pieces
            hot_table = (block_ids[:, None] == cluster_range[None, :]).astype(jnp.bfloat16)
            totals = totals + lax.dot_general(
                hot_table, block_x, (((0,), (0,)), ((), ())), preferred_element_type=jnp.float32
            )
            counts = counts + jnp.sum(hot_table, axis=0, dtype=jnp.float32)
            return ((totals, counts), None)

        start = (
            jnp.zeros((clusters, feat_width), jnp.float32),
            jnp.zeros((clusters,), jnp.float32),
        )
        result, unused = lax.scan(
            add_block, start, (row_blocks, cluster_ids.reshape(block_count, block_rows))
        )
        return result

    start_table = initial_centroids.reshape(clusters, feat_width).astype(jnp.float32)

    def update(earlier, cluster_ids):
        totals, counts = local_totals(cluster_ids)
        totals, counts = (
            lax.psum(totals.astype(jnp.bfloat16), "mem").astype(jnp.float32),
            lax.psum(counts.astype(jnp.bfloat16), "mem").astype(jnp.float32),
        )
        centre = (totals + PRIOR * earlier) / (counts[:, None] + PRIOR)
        return (centre, centre.astype(jnp.bfloat16))

    centre_one, rounded_one = update(start_table, ids_one)
    assigned = jnp.take(rounded_one, jnp.maximum(ids_one, 0), axis=0).astype(jnp.float32)
    first_local = (
        squares
        - 2.0 * jnp.sum(got_rows.astype(jnp.float32) * assigned, axis=1)
        + jnp.sum(assigned * assigned, axis=1)
    ) / feat_width
    centre_two, rounded_two = update(centre_one, ids_two)
    centre_squares = jnp.sum(jnp.square(rounded_two.astype(jnp.float32)), axis=1).reshape(
        group_codes, codes_two
    )
    code_range = jnp.arange(group_codes, dtype=jnp.int32)

    def score_block(pieces):
        block_x, block_offsets, block_sq = pieces
        raw = lax.dot_general(
            rounded_two, block_x, (((1,), (1,)), ((), ())), preferred_element_type=jnp.float32
        )
        raw = raw.reshape(group_codes, codes_two, block_rows)
        select = (block_offsets[None, :] == code_range[:, None]).astype(jnp.float32)
        inner = jnp.sum(raw * select[:, None, :], axis=0)
        norms = jnp.sum(centre_squares[:, :, None] * select[:, None, :], axis=0)
        return (block_sq[None, :] - 2.0 * inner + norms) / feat_width

    scored = lax.map(
        score_block,
        (
            row_blocks,
            offsets.reshape(block_count, block_rows),
            squares.reshape(block_count, block_rows),
        ),
    )
    all_local = jnp.transpose(scored, (1, 0, 2)).reshape(codes_two, slot_total)
    one_local = first_local[None, :]
    back_all, back_one = (
        lax.all_to_all(all_local, ("grp", "mem"), split_axis=1, concat_axis=1, tiled=True),
        lax.all_to_all(one_local, ("grp", "mem"), split_axis=1, concat_axis=1, tiled=True),
    )
    distances = jnp.take(back_all, slot_index, axis=1)
    first_distance = jnp.take(back_one[0], slot_index, axis=0)
    return (distances, first_distance)


def solution(mesh):
    placed = (
        P(("grp", "mem"), None),
        P("grp", None, None),
        P(("grp", "mem"), None),
        P(("grp", "mem")),
        P(("grp", "mem")),
        P(("grp", "mem")),
    )
    return jax.shard_map(
        body,
        mesh=mesh,
        in_specs=placed,
        out_specs=(P(None, ("grp", "mem")), P(("grp", "mem"))),
        check_vma=False,
    )
```

profile of v0, /device:TPU:1, one launch (start us, length us, event | category | flops | bytes accessed | tf_op | source)
XLA Modules:
  0.0 316.1 jit_solution(4877060308252872345)
XLA Ops:
  7.2 0.8 copy.30
  8.0 0.2 fusion.31
  8.3 0.9 fusion.30
  9.2 0.7 and_reduce_fusion
  9.9 0.7 pad_add_fusion
  10.6 0.1 copy.32
  10.8 1.9 scatter_custom_fusion.1
  12.7 0.3 copy.33
  13.0 0.2 all_to_all.28
  13.2 0.8 copy.34
  14.0 11.5 %all-to-all-start.1 = ((s32[128,12,3]{1,2,0:T(4,128)}), s32[128,12,3]{1,2,0:T(4,128)S(1)}, u32[]{:S(2)}, u32[]{:S(2)}) async-start(s32[128,12,3]{1,2,0:T(4,128)} %copy.34), calls=%async_computation.1 | async-start | bytes 524288 | tf_op jit(solution)/shard_map/all_to_all | solution.py:37
  25.5 3.9 %scatter_custom_fusion = bf16[1536,768]{1,0:T(8,128)(2,1)S(1)} fusion(s32[512]{0:T(512)S(1)} %bitcast.83, bf16[512,768]{1,0:T(8,128)(2,1)} %param.12, bf16[]{:T(256)} %constant.106.clone.1), kind=kCustom, calls=%fused_computation.53 | custom fusion | bytes 2359808 | tf_op jit(solution)/shard_map/scatter | solution.py:32
  29.4 2.4 all_to_all.26
  31.8 5.1 %all-to-all-done.1 = s32[128,12,3]{1,2,0:T(4,128)S(1)} async-done(((s32[128,12,3]{1,2,0:T(4,128)}), s32[128,12,3]{1,2,0:T(4,128)S(1)}, u32[]{:S(2)}, u32[]{:S(2)}) %all-to-all-start.1) | async-done | bytes 18464 | tf_op jit(solution)/shard_map/all_to_all | solution.py:37
  37.0 4.6 %all-to-all-start = ((bf16[128,12,768]{2,1,0:T(8,128)(2,1)}), bf16[128,12,768]{2,1,0:T(8,128)(2,1)S(1)}, u32[]{:S(2)}, u32[]{:S(2)}) async-start(bf16[128,12,768]{2,1,0:T(8,128)(2,1)} %all_to_all.26), calls=%async_computation | async-start | bytes 6291456 | tf_op jit(solution)/shard_map/all_to_all | solution.py:36
  41.6 0.2 all-reduce.4.cloned.1.call-start
  41.9 0.7 copy.35
  42.6 1.1 all_to_all.30
  43.8 38.0 %all-to-all-done = bf16[128,12,768]{2,1,0:T(8,128)(2,1)S(1)} async-done(((bf16[128,12,768]{2,1,0:T(8,128)(2,1)}), bf16[128,12,768]{2,1,0:T(8,128)(2,1)S(1)}, u32[]{:S(2)}, u32[]{:S(2)}) %all-to-all-start) | async-done | bytes 2359328 | tf_op jit(solution)/shard_map/all_to_all | solution.py:36
  81.8 2.6 reshape.197
  84.4 12.5 %while.38 = (s32[]{:T(128)}, f32[1300,768]{1,0:T(8,128)}, f32[1300]{0:T(1024)S(1)}, s32[2,768]{1,0:T(2,128)S(1)}, bf16[2,768,768]{2,1,0:T(8,128)(2,1)}, /*index=5*/s32[]{:T(128)}, s32[]{:T(128)}) while((s32[]{:T(128)}, f32[1300,768]{1,0:T(8,128)}, f32[1300]{0:T(1024)S(1)}, s32[2,768]{1,0:T(2,128)S(1)}, ...), condition=%wide.region_8.9_spmd.clone, body=%wide.region_6.8_spmd.clone.sunk | while | flops 1540532480 | bytes 9212828 | solution.py:65
  84.4 5.1 %select_add_fusion.8 = f32[1300,768]{1,0:T(8,128)} fusion(f32[1300,768]{1,0:T(8,128)} %get-tuple-element.411, s32[768]{0:T(1024)S(1)} %dynamic-slice_reduce_fusion.10, pred[]{:T(512)S(6)} %compare.6, bf16[2,768,768]{2,1,0:T(8,128)(2,1)} %get-tuple-element.421, s32[]{:T(128)} %get-tuple-element.410), kind=kOutput, calls=%fused_computation.25.clone.1 | convolution fusion | flops 1536537600 | bytes 9182721 | tf_op jit(solution)/shard_map/while/body/eval_jaxpr/dot_general | solution.py:55
  89.5 0.5 convert_reduce_fusion.4
  90.1 6.3 %select_add_fusion.8 = f32[1300,768]{1,0:T(8,128)} fusion(f32[1300,768]{1,0:T(8,128)} %get-tuple-element.411, s32[768]{0:T(1024)S(1)} %dynamic-slice_reduce_fusion.10, pred[]{:T(512)S(6)} %compare.6, bf16[2,768,768]{2,1,0:T(8,128)(2,1)} %get-tuple-element.421, s32[]{:T(128)} %get-tuple-element.410), kind=kOutput, calls=%fused_computation.25.clone.1 | convolution fusion | flops 1536537600 | bytes 9182721 | tf_op jit(solution)/shard_map/while/body/eval_jaxpr/dot_general | solution.py:55
  96.4 0.5 convert_reduce_fusion.4
  96.9 3.7 %convert_element_type.75 = bf16[1300,768]{1,0:T(8,128)(2,1)} convert(f32[1300,768]{1,0:T(8,128)} %get-tuple-element.110) | non-fusion elementwise | flops 998400 | bytes 5990400 | tf_op jit(solution)/shard_map/convert_element_type | solution.py:75
  100.7 10.9 %while.39 = (s32[]{:T(128)}, f32[1300,768]{1,0:T(8,128)}, f32[1300]{0:T(1024)S(1)}, s32[2,768]{1,0:T(2,128)S(1)}, bf16[2,768,768]{2,1,0:T(8,128)(2,1)S(1)}, /*index=5*/s32[]{:T(128)}, s32[]{:T(128)}) while((s32[]{:T(128)}, f32[1300,768]{1,0:T(8,128)}, f32[1300]{0:T(1024)S(1)}, s32[2,768]{1,0:T(2,128)S(1)}, ...), condition=%wide.region_12.13_spmd.clone, body=%wide.region_10.12_spmd.clone.sunk | while | flops 1540532480 | bytes 9201056 | solution.py:65
  100.7 3.8 %select_add_fusion.10 = f32[1300,768]{1,0:T(8,128)} fusion(f32[1300,768]{1,0:T(8,128)} %get-tuple-element.390, s32[768]{0:T(1024)S(1)} %dynamic-slice_reduce_fusion.11, pred[]{:T(512)S(6)} %compare.7, bf16[2,768,768]{2,1,0:T(8,128)(2,1)S(1)} %get-tuple-element.400, s32[]{:T(128)} %get-tuple-element.389), kind=kOutput, calls=%fused_computation.36.clone.1 | convolution fusion | flops 1536537600 | bytes 9170949 | tf_op jit(solution)/shard_map/while/body/eval_jaxpr/dot_general | solution.py:55
  104.5 0.5 convert_reduce_fusion.5
  105.1 6.0 %select_add_fusion.10 = f32[1300,768]{1,0:T(8,128)} fusion(f32[1300,768]{1,0:T(8,128)} %get-tuple-element.390, s32[768]{0:T(1024)S(1)} %dynamic-slice_reduce_fusion.11, pred[]{:T(512)S(6)} %compare.7, bf16[2,768,768]{2,1,0:T(8,128)(2,1)S(1)} %get-tuple-element.400, s32[]{:T(128)} %get-tuple-element.389), kind=kOutput, calls=%fused_computation.36.clone.1 | convolution fusion | flops 1536537600 | bytes 9170949 | tf_op jit(solution)/shard_map/while/body/eval_jaxpr/dot_general | solution.py:55
  111.1 0.5 convert_reduce_fusion.5
  111.6 3.8 %convert_element_type.77 = bf16[1300,768]{1,0:T(8,128)(2,1)} convert(f32[1300,768]{1,0:T(8,128)} %get-tuple-element.111) | non-fusion elementwise | flops 998400 | bytes 5990400 | tf_op jit(solution)/shard_map/convert_element_type | solution.py:75
  115.4 2.2 convert_multiply_fusion.2
  117.6 5.0 %mul.91 = f32[1300,768]{1,0:T(8,128)} reshape(f32[13,100,768]{2,1,0:T(8,128)} %convert_multiply_fusion.2) | data formatting | bytes 7987200 | tf_op jit(solution)/shard_map/mul | solution.py:78
  122.7 0.1 broadcast_in_dim.72
  122.9 32.6 %all-reduce = (bf16[1300]{0:T(1024)(128)(2,1)S(1)}, bf16[1300]{0:T(1024)(128)(2,1)S(1)}) all-reduce(bf16[1300]{0:T(1024)(128)(2,1)S(1)} %convert_element_type.80, bf16[1300]{0:T(1024)(128)(2,1)S(1)} %convert_element_type.82), channel_id=1, replica_groups=mesh['grp'=8,'mem'=16] {'mem'}, use_global_device_ids=true, to_apply=%region_14.15 | all-reduce | flops 2600 | bytes 10400 | tf_op jit(solution)/shard_map/psum | solution.py:76
  155.5 60.2 %all-reduce.4.cloned.1.call-done = (bf16[1300,768]{1,0:T(8,128)(2,1)}, bf16[1300,768]{1,0:T(8,128)(2,1)}) async-done(((bf16[1300,768]{1,0:T(8,128)(2,1)}, bf16[1300,768]{1,0:T(8,128)(2,1)}), (bf16[1300,768]{1,0:T(8,128)(2,1)}, bf16[1300,768]{1,0:T(8,128)(2,1)})) %all-reduce.4.cloned.1.call-update) | async-done | bytes 3993616 | tf_op jit(solution)/shard_map/psum | solution.py:75
  215.7 5.1 %multiply_reduce_fusion.3 = (f32[1300]{0:T(1024)S(1)}, bf16[1300,768]{1,0:T(8,128)(2,1)}, bf16[1300,768]{1,0:T(8,128)(2,1)S(1)}) fusion(f32[1300]{0:T(1024)S(1)} %get-tuple-element.235, f32[1300]{0:T(1024)S(1)} %get-tuple-element.236, f32[1300,768]{1,0:T(8,128)} %mul.91, bf16[1300,768]{1,0:T(8,128)(2,1)} %get-tuple-element.224, ...), kind=kLoop, calls=%fused_computation.50 | loop fusion | flops 11979500 | bytes 11996400 | tf_op jit(solution)/shard_map/reduce_sum | solution.py:89
  220.8 5.6 %gather_fusion.1 = bf16[1536,768]{1,0:T(8,128)(2,1)} fusion(bf16[1300,768]{1,0:T(8,128)(2,1)S(1)} %get-tuple-element.232, s32[2048]{0:T(1024)S(1)} %pad_clamp_fusion), kind=kCustom, calls=%fused_computation.1 | custom fusion | bytes 4724736 | tf_op jit(solution)/shard_map/jit(_take)/gather | solution.py:82
  226.4 5.0 %gather.16 = bf16[128,12,768]{2,1,0:T(8,128)(2,1)} reshape(bf16[1536,768]{1,0:T(8,128)(2,1)} %gather_fusion.1) | data formatting | bytes 4718592 | tf_op jit(solution)/shard_map/jit(_take)/gather | solution.py:82
  231.4 2.5 multiply_reduce_fusion.2
  234.1 4.1 %fusion.25 = (f32[128,12]{1,0:T(8,128)S(1)}, f32[128,12]{1,0:T(8,128)S(1)}) fusion(bf16[128,12,768]{2,1,0:T(8,128)(2,1)S(1)} %copy-done.1, bf16[128,12,768]{2,1,0:T(8,128)(2,1)} %gather.16, pred[128,12]{1,0:T(8,128)(4,1)S(1)} %broadcast_in_dim.72), kind=kLoop, calls=%fused_computation.47 | loop fusion | flops 8254464 | bytes 4732416 | tf_op jit(solution)/shard_map/reduce_sum | solution.py:85
  238.3 0.6 fusion.34
  238.9 8.1 %all-to-all-start.3 = ((f32[1,128,12]{2,0,1:T(1,128)}), f32[1,128,12]{2,0,1:T(1,128)S(1)}, u32[]{:S(2)}, u32[]{:S(2)}) async-start(f32[1,128,12]{2,0,1:T(1,128)} %bitcast.13), calls=%async_computation.3 | async-start | bytes 131072 | tf_op jit(solution)/shard_map/all_to_all | solution.py:117
  247.1 29.0 %while.40 = (s32[]{:T(128)}, f32[2,100,768]{2,1,0:T(8,128)}, f32[2,768]{1,0:T(2,128)S(1)}, bf16[2,768,768]{2,1,0:T(8,128)(2,1)}, bf16[1300,768]{1,0:T(8,128)(2,1...) while((s32[]{:T(128)}, f32[2,100,768]{2,1,0:T(8,128)}, ...), condition=%wide.wide.region_20.21_spmd.clone, body=%wide.wide.region_17.20_spmd.clone.sunk | while | flops 1537709568 | bytes 25750256 | solution.py:105
  247.1 5.6 %convolution_bitcast_fusion.3 = f32[1300,768]{1,0:T(8,128)} fusion(bf16[1300,768]{1,0:T(8,128)(2,1)} %get-tuple-element.446, bf16[2,768,768]{2,1,0:T(8,128)(2,1)} %get-tuple-element.445, s32[]{:T(128)} %get-tuple-element.433), kind=kOutput, calls=%fused_computation.10.clone.clone.1 | convolution fusion | flops 1533542400 | bytes 7176704 | tf_op jit(solution)/shard_map/while/body/eval_jaxpr/dot_general | solution.py:96
  252.7 5.0 %reshape.265 = f32[13,100,768]{2,1,0:T(8,128)} reshape(f32[1300,768]{1,0:T(8,128)} %convolution_bitcast_fusion.3) | data formatting | bytes 7987200 | tf_op jit(solution)/shard_map/while/body/eval_jaxpr/reshape | solution.py:99
  257.7 3.0 multiply_reduce_fusion.6
  260.8 0.8 copy-done.5
  261.6 5.6 %convolution_bitcast_fusion.3 = f32[1300,768]{1,0:T(8,128)} fusion(bf16[1300,768]{1,0:T(8,128)(2,1)} %get-tuple-element.446, bf16[2,768,768]{2,1,0:T(8,128)(2,1)} %get-tuple-element.445, s32[]{:T(128)} %get-tuple-element.433), kind=kOutput, calls=%fused_computation.10.clone.clone.1 | convolution fusion | flops 1533542400 | bytes 7176704 | tf_op jit(solution)/shard_map/while/body/eval_jaxpr/dot_general | solution.py:96
  267.2 5.0 %reshape.265 = f32[13,100,768]{2,1,0:T(8,128)} reshape(f32[1300,768]{1,0:T(8,128)} %convolution_bitcast_fusion.3) | data formatting | bytes 7987200 | tf_op jit(solution)/shard_map/while/body/eval_jaxpr/reshape | solution.py:99
  272.2 3.0 multiply_reduce_fusion.6
  275.3 0.8 copy-done.5
  276.1 1.4 copy.36
  277.5 1.1 all_to_all.31
  278.6 9.8 %all-to-all-start.2 = ((f32[100,128,12]{0,2,1:T(8,128)}), f32[100,128,12]{0,2,1:T(8,128)S(1)}, u32[]{:S(2)}, u32[]{:S(2)}) async-start(f32[100,128,12]{0,2,1:T(8,128)} %all_to_all.31), calls=%async_computation.2 | async-start | bytes 2097152 | tf_op jit(solution)/shard_map/all_to_all | solution.py:116
  288.3 0.5 broadcast.254
  288.8 0.8 reduce.25
  289.8 3.1 gather_fusion.2
  292.9 0.6 broadcast_select_fusion
  293.5 13.6 %all-to-all-done.2 = f32[100,128,12]{0,2,1:T(8,128)S(1)} async-done(((f32[100,128,12]{0,2,1:T(8,128)}), f32[100,128,12]{0,2,1:T(8,128)S(1)}, u32[]{:S(2)}, u32[]{:S(2)}) %all-to-all-start.2) | async-done | bytes 614432 | tf_op jit(solution)/shard_map/all_to_all | solution.py:116
  307.2 1.0 gather_fusion
  308.3 0.1 select_bitcast_fusion
  308.4 0.8 copy.38
  (63 shorter events, 1.1 us)
Async XLA Ops:
  14.0 22.9 %all-to-all-start.1 = ((s32[128,12,3]{1,2,0:T(4,128)}), s32[128,12,3]{1,2,0:T(4,128)S(1)}, u32[]{:S(2)}, u32[]{:S(2)}) async-start(s32[128,12,3]{1,2,0:T(4,128)} %copy.34), calls=%async_computation.1 | async-start | bytes 524288 | tf_op jit(solution)/shard_map/all_to_all | solution.py:37
  37.0 44.8 %all-to-all-start = ((bf16[128,12,768]{2,1,0:T(8,128)(2,1)}), bf16[128,12,768]{2,1,0:T(8,128)(2,1)S(1)}, u32[]{:S(2)}, u32[]{:S(2)}) async-start(bf16[128,12,768]{2,1,0:T(8,128)(2,1)} %all_to_all.26), calls=%async_computation | async-start | bytes 6291456 | tf_op jit(solution)/shard_map/all_to_all | solution.py:36
  41.6 174.1 %all-reduce.4.cloned.1.call-start = ((), (), s32[]{:S(2)}) async-start(), calls=%async_computation.4 | async-start | bytes 8011776 | tf_op jit(solution)/shard_map/psum | solution.py:75
  81.8 2.6 copy-start
  96.9 3.8 %copy-start.2 = (bf16[2,768,768]{2,1,0:T(8,128)(2,1)S(1)}, bf16[2,768,768]{2,1,0:T(8,128)(2,1)}, u32[]{:S(2)}) copy-start(bf16[2,768,768]{2,1,0:T(8,128)(2,1)} %get-tuple-element.462) | copy-start | bytes 7077892
  111.6 3.8 %copy-start.3 = (bf16[13,100,768]{2,1,0:T(8,128)(2,1)S(1)}, bf16[13,100,768]{2,1,0:T(8,128)(2,1)}, u32[]{:S(2)}) copy-start(bf16[13,100,768]{2,1,0:T(8,128)(2,1)} %param.13) | copy-start | bytes 5990404
  220.8 26.2 %copy-start.6 = (f32[1300]{0:T(1024)}, f32[1300]{0:T(1024)S(1)}, u32[]{:S(2)}) copy-start(f32[1300]{0:T(1024)S(1)} %get-tuple-element.430) | copy-start | bytes 15604
  226.4 7.7 %copy-start.1 = (bf16[128,12,768]{2,1,0:T(8,128)(2,1)S(1)}, bf16[128,12,768]{2,1,0:T(8,128)(2,1)}, u32[]{:S(2)}) copy-start(bf16[128,12,768]{2,1,0:T(8,128)(2,1)} %copy-done) | copy-start | bytes 7077892
  238.9 39.6 %all-to-all-start.3 = ((f32[1,128,12]{2,0,1:T(1,128)}), f32[1,128,12]{2,0,1:T(1,128)S(1)}, u32[]{:S(2)}, u32[]{:S(2)}) async-start(f32[1,128,12]{2,0,1:T(1,128)} %bitcast.13), calls=%async_computation.3 | async-start | bytes 131072 | tf_op jit(solution)/shard_map/all_to_all | solution.py:117
  257.7 3.0 copy-start.4
  260.8 0.8 copy-start.5
  272.2 3.0 copy-start.4
  275.3 0.8 copy-start.5
  278.6 28.6 %all-to-all-start.2 = ((f32[100,128,12]{0,2,1:T(8,128)}), f32[100,128,12]{0,2,1:T(8,128)S(1)}, u32[]{:S(2)}, u32[]{:S(2)}) async-start(f32[100,128,12]{0,2,1:T(8,128)} %all_to_all.31), calls=%async_computation.2 | async-start | bytes 2097152 | tf_op jit(solution)/shard_map/all_to_all | solution.py:116
Sparse Core Ops, SparseCore 0:
  115.5 100.1 all-reduce.3
where the time goes:
time: 317 us; the launch traced here: 316 us
  waiting for transfers between devices  117 us (37%)
  local copies, waits for them, and re-layouts  50.9 us (16%)
  other arithmetic  34.4 us (11%)
  starting transfers between devices  34.2 us (11%)
  blocking collectives  32.6 us (10%)
  matrix products  32.4 us (10%)
  between operations  14.4 us (5%)
    psum x1, waiting for transfers between devices, update(): lax.psum(totals.astype(jnp.bfloat16), 'mem').astype(jnp.float32)  60.2 us
    all_to_all x1, waiting for transfers between devices, body(): lax.all_to_all(send_rows, ('grp', 'mem'), split_axis=0, concat_axis=0, ti...  38 us
    psum x1, blocking collectives, update(): lax.psum(counts.astype(jnp.bfloat16), 'mem').astype(jnp.float32)  32.6 us
    dot_general x4, matrix products, add_block(): lax.dot_general(hot_table, block_x, (((0,), (0,)), ((), ())), preferred_e...  21.2 us
    all_to_all x1, waiting for transfers between devices, body(): lax.all_to_all(all_local, ('grp', 'mem'), split_axis=1, concat_axis=1, ti...  13.6 us
    all_to_all x1, starting transfers between devices, body(): lax.all_to_all(send_labels, ('grp', 'mem'), split_axis=0, concat_axis=0,...  11.5 us
    dot_general x2, matrix products, score_block(): lax.dot_general(rounded_two, block_x, (((1,), (1,)), ((), ())), preferred...  11.2 us
    gather x2, local copies, waits for them, and re-layouts, body(): jnp.take(rounded_one, jnp.maximum(ids_one, 0), axis=0).astype(jnp.float32)  10.6 us
  transfers between devices with their start and end apart: 5, of which 4 were waited for; matrix products, arithmetic and copies ran while one was open for 15% of the time, Pallas kernels for 0%

commit v1 on v0

--- a/solution.py
+++ b/solution.py
@@ -1,9 +1,210 @@
 import jax
 import jax.numpy as jnp
 from jax import lax
+from jax.experimental import pallas as pl
+from jax.experimental.pallas import tpu as pltpu
 from jax.sharding import PartitionSpec as P
 
 PRIOR = 16
+SLOTS_GROUP = 128
+SLOTS_CODE = 96
+LANES = 128
+OFFSET, FIRST, SECOND, LIVE, FULL = 0, 1, 2, 3, 4
+NT = (((1,), (1,)), ((), ()))
+VMEM_LIMIT = 48 * 1024 * 1024
+
+
+def iota(shape, dim):
+    return lax.broadcasted_iota(jnp.int32, shape, dim)
+
+
+def hot(condition):
+    return jnp.where(condition, 1.0, 0.0).astype(jnp.bfloat16)
+
+
+def dot(a, b):
+    return jnp.dot(a, b, preferred_element_type=jnp.float32)
+
+
+def dot_nt(a, b):
+    return lax.dot_general(a, b, NT, preferred_element_type=jnp.float32)
+
+
+def three_terms(values):
+    high = values.astype(jnp.bfloat16)
+    rest = values - high.astype(jnp.float32)
+    middle = rest.astype(jnp.bfloat16)
+    low = (rest - middle.astype(jnp.float32)).astype(jnp.bfloat16)
+    return high, middle, low
+
+
+def call(kernel, out_shape, args, out_memory=None):
+    count = len(args)
+    in_specs = [pl.BlockSpec(memory_space=pltpu.VMEM)] * count
+    out_specs = out_memory or [pl.BlockSpec(memory_space=pltpu.VMEM)] * len(out_shape)
+    return pl.pallas_call(
+        kernel,
+        out_shape=out_shape,
+        in_specs=in_specs,
+        out_specs=out_specs,
+        compiler_params=pltpu.CompilerParams(vmem_limit_bytes=VMEM_LIMIT),
+    )(*args)
+
+
+def pack_kernel(member_count, owner_ref, offset_ref, first_ref, second_ref, x_ref, send_ref, slot_ref):
+    rows, feat = x_ref.shape
+    groups = send_ref.shape[0] // SLOTS_GROUP
+    group = owner_ref[...] // member_count
+    member = iota((16, rows), 0) == group
+    hot_group = hot(member)
+    before = hot(iota((rows, rows), 0) < iota((rows, rows), 1))
+    rank = jnp.sum(jnp.where(member, dot(hot_group, before), 0.0), axis=0, keepdims=True)
+    rank = rank.astype(jnp.int32)
+    fits = rank < SLOTS_GROUP
+    full = jnp.max(jnp.where(fits, 0.0, 1.0))
+    slot = jnp.where(fits, group * SLOTS_GROUP + rank, -1)
+    slot_ref[...] = slot
+    kind = iota((LANES, rows), 0)
+    labels = jnp.where(kind == OFFSET, offset_ref[...], 0)
+    labels = jnp.where(kind == FIRST, first_ref[...], labels)
+    labels = jnp.where(kind == SECOND, second_ref[...], labels)
+    labels = jnp.where(kind == LIVE, 1, labels)
+    labels = labels.astype(jnp.float32).astype(jnp.bfloat16)
+    full_column = jnp.where(iota((SLOTS_GROUP, LANES), 1) == FULL, full, 0.0)
+    x = x_ref[...]
+    for block in range(groups):
+        begin = block * SLOTS_GROUP
+        place = hot(iota((SLOTS_GROUP, rows), 0) + begin == slot)
+        send_ref[begin : begin + SLOTS_GROUP, :feat] = dot(place, x).astype(jnp.bfloat16)
+        send_ref[begin : begin + SLOTS_GROUP, feat:] = (dot_nt(place, labels) + full_column).astype(
+            jnp.bfloat16
+        )
+
+
+def relay_kernel(got_ref, send_ref, place_ref):
+    total, width = got_ref.shape
+    feat = width - LANES
+    labels = got_ref[:, feat:]
+    columns = labels.astype(jnp.float32)
+    full = jnp.max(jnp.where(iota((total, LANES), 1) == FULL, columns, 0.0))
+    turn = hot(iota((16, LANES), 0) == iota((16, LANES), 1))
+    across = dot_nt(turn, labels)
+    lane_code = across[OFFSET : OFFSET + 1]
+    lane_live = across[LIVE : LIVE + 1] > 0.5
+    member = (iota((16, total), 0).astype(jnp.float32) == lane_code) & lane_live
+    hot_code = hot(member)
+    before = hot(iota((LANES, LANES), 0) < iota((LANES, LANES), 1))
+    base = jnp.zeros((16, 1), jnp.float32)
+    ranks = []
+    for begin in range(0, total, LANES):
+        piece = hot_code[:, begin : begin + LANES]
+        ranks.append(dot(piece, before) + base)
+        base = base + jnp.sum(piece.astype(jnp.float32), axis=1, keepdims=True)
+    rank = jnp.concatenate(ranks, axis=1)
+    rank = jnp.sum(jnp.where(member, rank, 0.0), axis=0, keepdims=True)
+    fits = rank < SLOTS_CODE
+    full = jnp.maximum(full, jnp.max(jnp.where(lane_live & ~fits, 1.0, 0.0)))
+    place = jnp.where(lane_live & fits, lane_code * SLOTS_CODE + rank, -1.0).astype(jnp.int32)
+    column_member = (iota((total, LANES), 1).astype(jnp.float32) == columns[:, OFFSET : OFFSET + 1]) & (
+        columns[:, LIVE : LIVE + 1] > 0.5
+    )
+    column_hot = hot(column_member)
+    after = hot(iota((LANES, LANES), 0) > iota((LANES, LANES), 1))
+    base = jnp.zeros((1, LANES), jnp.float32)
+    for begin in range(0, total, LANES):
+        piece = column_hot[begin : begin + LANES]
+        counted = dot(after, piece) + base
+        base = base + jnp.sum(piece.astype(jnp.float32), axis=0, keepdims=True)
+        chosen = column_member[begin : begin + LANES]
+        own = jnp.sum(jnp.where(chosen, counted, 0.0), axis=1, keepdims=True)
+        live = columns[begin : begin + LANES, LIVE : LIVE + 1] > 0.5
+        code = columns[begin : begin + LANES, OFFSET : OFFSET + 1]
+        own = jnp.where(live & (own < SLOTS_CODE), code * SLOTS_CODE + own, -1.0)
+        place_ref[begin : begin + LANES, :] = own.astype(jnp.int32)
+    got = got_ref[...]
+    is_full = iota((SLOTS_CODE, LANES), 1) == FULL
+    blocks = send_ref.shape[0] // SLOTS_CODE
+    for block in range(blocks):
+        begin = block * SLOTS_CODE
+        chosen = hot(iota((SLOTS_CODE, total), 0) + begin == place)
+        moved = dot(chosen, got)
+        send_ref[begin : begin + SLOTS_CODE, :feat] = moved[:, :feat].astype(jnp.bfloat16)
+        send_ref[begin : begin + SLOTS_CODE, feat:] = jnp.where(is_full, full, moved[:, feat:]).astype(
+            jnp.bfloat16
+        )
+
+
+def code_kernel(got_ref, start_ref, out_ref, start):
+    total, width = got_ref.shape
+    feat = width - LANES
+    codes_two = start_ref.shape[0]
+    start[...] = jnp.zeros_like(start)
+    start[0:codes_two, :] = start_ref[...].astype(jnp.float32)
+    x = got_ref[:, :feat]
+    labels = got_ref[:, feat:]
+    columns = labels.astype(jnp.float32)
+    lane = iota((total, LANES), 1)
+    full = jnp.max(jnp.where(lane == FULL, columns, 0.0))
+    turn = hot(iota((16, LANES), 0) == iota((16, LANES), 1))
+    across = dot_nt(turn, labels)
+    live = across[LIVE : LIVE + 1] > 0.5
+    cluster = iota((LANES, total), 0).astype(jnp.float32)
+
+    def update(earlier, assigned):
+        member = hot((cluster == assigned) & live)
+        totals = dot(member, x)
+        counts = jnp.sum(member.astype(jnp.float32), axis=1, keepdims=True)
+        return (totals + PRIOR * earlier) / (counts + PRIOR)
+
+    diagonal = iota((LANES, LANES), 0) == iota((LANES, LANES), 1)
+
+    def squares_of(rounded):
+        wide = rounded.astype(jnp.float32)
+        down = jnp.sum(wide * wide, axis=1, keepdims=True)
+        return jnp.sum(jnp.where(diagonal, down, 0.0), axis=0, keepdims=True)
+
+    centre_one = update(start[...], across[FIRST : FIRST + 1])
+    rounded_one = centre_one.astype(jnp.bfloat16)
+    centre_two = update(centre_one, across[SECOND : SECOND + 1])
+    rounded_two = centre_two.astype(jnp.bfloat16)
+    squares_one = squares_of(rounded_one)
+    squares_two = squares_of(rounded_two)
+    wide_x = x.astype(jnp.float32)
+    squares = jnp.sum(wide_x * wide_x, axis=1, keepdims=True)
+    near = (squares - 2.0 * dot_nt(x, rounded_one) + squares_one) / feat
+    near = jnp.sum(
+        jnp.where(lane.astype(jnp.float32) == columns[:, FIRST : FIRST + 1], near, 0.0),
+        axis=1,
+        keepdims=True,
+    )
+    score = (squares - 2.0 * dot_nt(x, rounded_two) + squares_two) / feat
+    score = jnp.where(lane == codes_two, near, score)
+    out_ref[...] = jnp.where(lane > codes_two, full, score)
+
+
+def unrelay_kernel(got_ref, place_ref, out_ref):
+    total = got_ref.shape[0]
+    got = got_ref[...]
+    full = jnp.max(got[:, LANES - 1 :])
+    terms = jnp.concatenate(three_terms(got), axis=1)
+    for begin in range(0, out_ref.shape[0], LANES):
+        chosen = hot(iota((LANES, total), 1) == place_ref[begin : begin + LANES, :])
+        moved = dot(chosen, terms)
+        moved = moved[:, :LANES] + (moved[:, LANES : 2 * LANES] + moved[:, 2 * LANES :])
+        out_ref[begin : begin + LANES, :] = jnp.where(iota((LANES, LANES), 1) == LANES - 1, full, moved)
+
+
+def unpack_kernel(got_ref, slot_ref, all_ref, one_ref, full_ref):
+    total = got_ref.shape[0]
+    rows = slot_ref.shape[1]
+    codes_two = all_ref.shape[0]
+    got = got_ref[...]
+    full_ref[0, 0] = (jnp.max(got[:, LANES - 1 :]) > 0.5).astype(jnp.int32)
+    high, middle, low = three_terms(got.T)
+    chosen = hot(iota((total, rows), 0) == slot_ref[...])
+    moved = dot(high, chosen) + (dot(middle, chosen) + dot(low, chosen))
+    all_ref[...] = moved[:codes_two]
+    one_ref[...] = moved[codes_two : codes_two + 1]
 
 
 def pick_block(total):
@@ -13,7 +214,7 @@
     return total
 
 
-def body(embeddings, initial_centroids, row_owner, prefix_offset, first_assign, second_assign):
+def general(embeddings, initial_centroids, row_owner, prefix_offset, first_assign, second_assign):
     row_count, feat_width = embeddings.shape
     group_codes = initial_centroids.shape[0]
     codes_two = initial_centroids.shape[1]
@@ -121,6 +322,81 @@
     return (distances, first_distance)
 
 
+def quick(embeddings, initial_centroids, row_owner, prefix_offset, first_assign, second_assign):
+    rows, feat = embeddings.shape
+    group_codes, codes_two = initial_centroids.shape[:2]
+    groups = lax.axis_size("grp")
+    members = lax.axis_size("mem")
+    width = feat + LANES
+    relay_total = groups * SLOTS_GROUP
+    code_total = members * SLOTS_CODE
+    shape = jax.ShapeDtypeStruct
+    send, slot = call(
+        lambda *refs: pack_kernel(members, *refs),
+        [shape((relay_total, width), jnp.bfloat16), shape((1, rows), jnp.int32)],
+        [
+            row_owner.reshape(1, rows),
+            prefix_offset.reshape(1, rows),
+            first_assign.reshape(1, rows),
+            second_assign.reshape(1, rows),
+            embeddings,
+        ],
+    )
+    got = lax.all_to_all(
+        send.reshape(groups, SLOTS_GROUP, width), "grp", split_axis=0, concat_axis=0, tiled=True
+    )
+    send, place = call(
+        relay_kernel,
+        [shape((code_total, width), jnp.bfloat16), shape((relay_total, 1), jnp.int32)],
+        [got.reshape(relay_total, width)],
+    )
+    got = lax.all_to_all(
+        send.reshape(members, SLOTS_CODE, width), "mem", split_axis=0, concat_axis=0, tiled=True
+    )
+    code = jnp.minimum(lax.axis_index("mem"), group_codes - 1)
+    start = lax.dynamic_index_in_dim(initial_centroids, code, 0, keepdims=False)
+    scored = pl.pallas_call(
+        code_kernel,
+        out_shape=shape((code_total, LANES), jnp.float32),
+        in_specs=[pl.BlockSpec(memory_space=pltpu.VMEM)] * 2,
+        out_specs=pl.BlockSpec(memory_space=pltpu.VMEM),
+        scratch_shapes=[pltpu.VMEM((LANES, feat), jnp.float32)],
+        compiler_params=pltpu.CompilerParams(vmem_limit_bytes=VMEM_LIMIT),
+    )(got.reshape(code_total, width), start)
+    back = lax.all_to_all(
+        scored.reshape(members, SLOTS_CODE, LANES), "mem", split_axis=0, concat_axis=0, tiled=True
+    )
+    (back,) = call(
+        unrelay_kernel,
+        [shape((relay_total, LANES), jnp.float32)],
+        [back.reshape(code_total, LANES), place],
+    )
+    back = lax.all_to_all(
+        back.reshape(groups, SLOTS_GROUP, LANES), "grp", split_axis=0, concat_axis=0, tiled=True
+    )
+    return call(
+        unpack_kernel,
+        [shape((codes_two, rows), jnp.float32), shape((1, rows), jnp.float32), shape((1, 1), jnp.int32)],
+        [back.reshape(relay_total, LANES), slot],
+        out_memory=[
+            pl.BlockSpec(memory_space=pltpu.VMEM),
+            pl.BlockSpec(memory_space=pltpu.VMEM),
+            pl.BlockSpec(memory_space=pltpu.SMEM),
+        ],
+    )
+
+
+def body(*inputs):
+    distances, first_distance, full = quick(*inputs)
+    return lax.cond(
+        full[0, 0] > 0,
+        lambda kept, given: general(*given),
+        lambda kept, given: kept,
+        (distances, first_distance[0]),
+        inputs,
+    )
+
+
 def solution(mesh):
     placed = (
         P(("grp", "mem"), None),

time: 317 us -> 140 us (0.44)
  waiting for transfers between devices: 117 us -> 48.2 us
  local copies, waits for them, and re-layouts: 50.9 us -> 3.17 us
  other arithmetic: 34.4 us -> 0 us
  matrix products: 32.4 us -> 0 us
  starting transfers between devices: 34.2 us -> 14.7 us
  Pallas kernels: 0 us -> 14.4 us
  blocking collectives: 32.6 us -> 44.6 us
    psum x1 -> x0, waiting for transfers between devices: 60.2 us -> none  [update(): lax.psum(totals.astype(jnp.bfloat16), 'mem').astype(jnp.float32)]
    all_to_all x0 -> x2, blocking collectives: none -> 44.6 us  [the longest x1 29.2 us: quick(): lax.all_to_all(send.reshape(groups, SLOTS_GROUP, width), 'grp', split_axi...]
    psum x1 -> x0, blocking collectives: 32.6 us -> none  [update(): lax.psum(counts.astype(jnp.bfloat16), 'mem').astype(jnp.float32)]
    dot_general x6 -> x0, matrix products: 32.4 us -> none  [the longest x4 21.2 us: add_block(): lax.dot_general(hot_table, block_x, (((0,), (0,)), ((), ())), preferred_e...]
    reduce_sum x10 -> x0, other arithmetic: 20.5 us -> none  [the longest x2 5.9 us: score_block(): inner = jnp.sum(raw * select[:, None, :], axis=0)]
    all_to_all x4 -> x2, starting transfers between devices: 34 us -> 14.7 us  [the longest x1 7.77 us: quick(): lax.all_to_all(send.reshape(members, SLOTS_CODE, width), 'mem', split_axi...]
    gather x4 -> x0, local copies, waits for them, and re-layouts: 14.8 us -> none  [the longest x2 10.6 us: body(): jnp.take(rounded_one, jnp.maximum(ids_one, 0), axis=0).astype(jnp.float32)]
    pallas_call x0 -> x5, Pallas kernels: none -> 14.4 us  [the longest x4 11.8 us: call(): pl.pallas_call(kernel, out_shape=out_shape, in_specs=in_specs, out_specs=...]
  transfers between devices with their start and end apart: 5 -> 2, of which waited for: 4 -> 2; matrix products, arithmetic and copies ran while one was open for 15% -> 1% of each run, Pallas kernels for 0% -> 0%
where the time goes in v1:
time: 140 us
  waiting for transfers between devices  48.2 us (34%)
  blocking collectives  44.6 us (32%)
  between operations  14.8 us (11%)
  starting transfers between devices  14.7 us (10%)
  Pallas kernels  14.4 us (10%)
  local copies, waits for them, and re-layouts  3.17 us (2%)
    all_to_all x1, waiting for transfers between devices, quick(): lax.all_to_all(send.reshape(members, SLOTS_CODE, width), 'mem', split_axi...  38.7 us
    all_to_all x1, blocking collectives, quick(): lax.all_to_all(send.reshape(groups, SLOTS_GROUP, width), 'grp', split_axi...  29.2 us
    all_to_all x1, blocking collectives, quick(): lax.all_to_all(scored.reshape(members, SLOTS_CODE, LANES), 'mem', split_a...  15.4 us
    pallas_call x4, Pallas kernels, call(): pl.pallas_call(kernel, out_shape=out_shape, in_specs=in_specs, out_specs=...  11.8 us
    all_to_all x1, waiting for transfers between devices, quick(): lax.all_to_all(back.reshape(groups, SLOTS_GROUP, LANES), 'grp', split_axi...  9.48 us
    all_to_all x1, starting transfers between devices, quick(): lax.all_to_all(send.reshape(members, SLOTS_CODE, width), 'mem', split_axi...  7.77 us
    all_to_all x1, starting transfers between devices, quick(): lax.all_to_all(back.reshape(groups, SLOTS_GROUP, LANES), 'grp', split_axi...  6.89 us
  transfers between devices with their start and end apart: 2, of which 2 were waited for; matrix products, arithmetic and copies ran while one was open for 1% of the time, Pallas kernels for 0%

profile of v1, /device:TPU:1, one launch (start us, length us, event | category | flops | bytes accessed | tf_op | source)
XLA Modules:
  0.0 140.0 jit_solution(7490744443423565159)
XLA Ops:
  7.2 2.7 %shard_map.79 = (bf16[1024,896]{1,0:T(8,128)(2,1)S(1)}, s32[1,512]{1,0:T(1,128)S(1)}) custom-call(s32[1,512]{1,0:T(1,128)} %bitcast.102, s32[1,512]{1,0:T(1,128)} %bitcast.106, s32[1,512]{1,0:T(1,128)} %bitcast.108, s32[1,512]{1,0:T(1,128)} %bitcast.110, bf16[512,768]{1,0:T(8,128)(2,1)} %refs_4_.1), custom_call_target="tpu_custom_call" | custom-call | tf_op jit(solution)/shard_map/pallas_call | solution.py:45
  9.8 29.2 %all_to_all.50 = bf16[8,128,896]{2,1,0:T(8,128)(2,1)S(1)} all-to-all(bf16[8,128,896]{2,1,0:T(8,128)(2,1)S(1)} %bitcast.98), channel_id=1, replica_groups=mesh['grp'=8,'mem'=16] {'grp'}, dimensions={0} | all-to-all | bytes 3670016 | tf_op jit(solution)/shard_map/all_to_all | solution.py:345
  39.1 5.3 %shard_map.80 = (bf16[1536,896]{1,0:T(8,128)(2,1)S(1)}, s32[1024,1]{1,0:T(8,128)S(1)}) custom-call(bf16[1024,896]{1,0:T(8,128)(2,1)S(1)} %bitcast.93), custom_call_target="tpu_custom_call" | custom-call | tf_op jit(solution)/shard_map/pallas_call | solution.py:45
  44.3 0.0 copy-start
  44.3 1.5 %copy-done = bf16[1536,896]{1,0:T(8,128)(2,1)} copy-done((bf16[1536,896]{1,0:T(8,128)(2,1)}, bf16[1536,896]{1,0:T(8,128)(2,1)S(1)}, u32[]{:S(2)}) %copy-start) | copy-done | bytes 2752536
  45.9 7.8 %all-to-all-start.5 = ((bf16[16,96,896]{2,1,0:T(8,128)(2,1)}), bf16[16,96,896]{2,1,0:T(8,128)(2,1)S(1)}, u32[]{:S(2)}, u32[]{:S(2)}) async-start(bf16[16,96,896]{2,1,0:T(8,128)(2,1)} %bitcast.96), calls=%async_computation.5 | async-start | bytes 5505024 | tf_op jit(solution)/shard_map/all_to_all | solution.py:353
  53.7 0.9 dynamic-slice_bitcast_fusion.start_ref
  54.6 38.7 %all-to-all-done.5 = bf16[16,96,896]{2,1,0:T(8,128)(2,1)S(1)} async-done(((bf16[16,96,896]{2,1,0:T(8,128)(2,1)}), bf16[16,96,896]{2,1,0:T(8,128)(2,1)S(1)}, u32[]{:S(2)}, u32[]{:S(2)}) %all-to-all-start.5) | async-done | bytes 2752544 | tf_op jit(solution)/shard_map/all_to_all | solution.py:353
  93.3 0.0 copy-start.7
  93.3 0.0 copy-start.9
  93.3 0.0 copy-start.10
  93.3 0.0 copy-start.11
  93.3 2.6 %shard_map.81 = f32[1536,128]{1,0:T(8,128)S(1)} custom-call(bf16[1536,896]{1,0:T(8,128)(2,1)S(1)} %bitcast.92, bf16[100,768]{1,0:T(8,128)(2,1)S(1)} %dynamic-slice_bitcast_fusion.start_ref), custom_call_target="tpu_custom_call" | custom-call | tf_op jit(solution)/shard_map/pallas_call | solution.py:358
  95.9 15.4 %all_to_all.51 = f32[16,96,128]{2,1,0:T(8,128)S(1)} all-to-all(f32[16,96,128]{2,1,0:T(8,128)S(1)} %bitcast.95), channel_id=1, replica_groups=mesh['grp'=8,'mem'=16] {'mem'}, dimensions={0} | all-to-all | bytes 1572864 | tf_op jit(solution)/shard_map/all_to_all | solution.py:366
  111.3 2.7 %shard_map.82 = f32[1024,128]{1,0:T(8,128)} custom-call(f32[1536,128]{1,0:T(8,128)S(1)} %bitcast.94, s32[1024,1]{1,0:T(8,128)S(1)} %get-tuple-element.146.place_ref), custom_call_target="tpu_custom_call" | custom-call | tf_op jit(solution)/shard_map/pallas_call | solution.py:45
  114.0 6.9 %all-to-all-start.7 = ((f32[8,128,128]{2,1,0:T(8,128)}), f32[8,128,128]{2,1,0:T(8,128)S(1)}, u32[]{:S(2)}, u32[]{:S(2)}) async-start(f32[8,128,128]{2,1,0:T(8,128)} %bitcast.26), calls=%async_computation.7 | async-start | bytes 1048576 | tf_op jit(solution)/shard_map/all_to_all | solution.py:374
  120.9 9.5 %all-to-all-done.7 = f32[8,128,128]{2,1,0:T(8,128)S(1)} async-done(((f32[8,128,128]{2,1,0:T(8,128)}), f32[8,128,128]{2,1,0:T(8,128)S(1)}, u32[]{:S(2)}, u32[]{:S(2)}) %all-to-all-start.7) | async-done | bytes 524320 | tf_op jit(solution)/shard_map/all_to_all | solution.py:374
  130.4 1.2 shard_map.83
  132.2 0.0 copy-done.7
  132.2 0.0 copy-done.9
  132.2 0.0 copy-done.10
  132.2 0.0 copy-done.11
  132.2 0.3 conditional.1
  132.5 0.0 copy-start.12
  132.5 0.0 copy-start.13
  132.5 0.7 copy-done.12
  133.2 0.0 copy-done.13
Async XLA Ops:
  44.3 1.6 %copy-start = (bf16[1536,896]{1,0:T(8,128)(2,1)}, bf16[1536,896]{1,0:T(8,128)(2,1)S(1)}, u32[]{:S(2)}) copy-start(bf16[1536,896]{1,0:T(8,128)(2,1)S(1)} %get-tuple-element.145) | copy-start | bytes 8257540
  45.9 47.4 %all-to-all-start.5 = ((bf16[16,96,896]{2,1,0:T(8,128)(2,1)}), bf16[16,96,896]{2,1,0:T(8,128)(2,1)S(1)}, u32[]{:S(2)}, u32[]{:S(2)}) async-start(bf16[16,96,896]{2,1,0:T(8,128)(2,1)} %bitcast.96), calls=%async_computation.5 | async-start | bytes 5505024 | tf_op jit(solution)/shard_map/all_to_all | solution.py:353
  93.3 38.9 %copy-start.7 = (s32[512,1]{0,1:T(1,128)S(1)}, s32[512,1]{0,1:T(1,128)}, u32[]{:S(2)}) copy-start(s32[512,1]{0,1:T(1,128)} %param.16) | copy-start | bytes 6148
  93.3 38.9 %copy-start.9 = (s32[512]{0:T(512)S(1)}, s32[512]{0:T(512)}, u32[]{:S(2)}) copy-start(s32[512]{0:T(512)} %param.17) | copy-start | bytes 6148
  93.3 38.9 %copy-start.10 = (s32[512]{0:T(512)S(1)}, s32[512]{0:T(512)}, u32[]{:S(2)}) copy-start(s32[512]{0:T(512)} %param.18) | copy-start | bytes 6148
  93.3 38.9 %copy-start.11 = (s32[512]{0:T(512)S(1)}, s32[512]{0:T(512)}, u32[]{:S(2)}) copy-start(s32[512]{0:T(512)} %param.19) | copy-start | bytes 6148
  114.0 16.4 %all-to-all-start.7 = ((f32[8,128,128]{2,1,0:T(8,128)}), f32[8,128,128]{2,1,0:T(8,128)S(1)}, u32[]{:S(2)}, u32[]{:S(2)}) async-start(f32[8,128,128]{2,1,0:T(8,128)} %bitcast.26), calls=%async_computation.7 | async-start | bytes 1048576 | tf_op jit(solution)/shard_map/all_to_all | solution.py:374
  132.5 0.7 copy-start.12
  132.5 0.7 copy-start.13

commit v2 on v0

--- a/solution.py
+++ b/solution.py
@@ -1,9 +1,240 @@
 import jax
 import jax.numpy as jnp
 from jax import lax
+from jax.experimental import pallas as pl
+from jax.experimental.pallas import tpu as pltpu
 from jax.sharding import PartitionSpec as P
 
 PRIOR = 16
+BLOCK_RELAY = 72
+BLOCK_CODE = 160
+LANES = 128
+FIRST, SECOND, GROUP = 0, 1, 2
+NT = (((1,), (1,)), ((), ()))
+VMEM_LIMIT = 48 * 1024 * 1024
+
+
+def iota(shape, dim):
+    return lax.broadcasted_iota(jnp.int32, shape, dim)
+
+
+def hot(condition):
+    return jnp.where(condition, 1.0, 0.0).astype(jnp.bfloat16)
+
+
+def dot(a, b):
+    return jnp.dot(a, b, preferred_element_type=jnp.float32)
+
+
+def dot_nt(a, b):
+    return lax.dot_general(a, b, NT, preferred_element_type=jnp.float32)
+
+
+def three_terms(values):
+    high = values.astype(jnp.bfloat16)
+    rest = values - high.astype(jnp.float32)
+    middle = rest.astype(jnp.bfloat16)
+    low = (rest - middle.astype(jnp.float32)).astype(jnp.bfloat16)
+    return high, middle, low
+
+
+def call(kernel, out_shape, args, out_memory=None, in_memory=None, scratch=()):
+    vmem = pl.BlockSpec(memory_space=pltpu.VMEM)
+    return pl.pallas_call(
+        kernel,
+        out_shape=out_shape,
+        in_specs=in_memory or [vmem] * len(args),
+        out_specs=out_memory or [vmem] * len(out_shape),
+        scratch_shapes=scratch,
+        compiler_params=pltpu.CompilerParams(vmem_limit_bytes=VMEM_LIMIT),
+    )(*args)
+
+
+def rank_in_bin(member):
+    bins = hot(member)
+    before = hot(iota((LANES, LANES), 0) < iota((LANES, LANES), 1))
+    base = jnp.zeros((member.shape[0], 1), jnp.float32)
+    ranks = []
+    for begin in range(0, member.shape[1], LANES):
+        piece = bins[:, begin : begin + LANES]
+        ranks.append(dot(piece, before) + base)
+        base = base + jnp.sum(piece.astype(jnp.float32), axis=1, keepdims=True)
+    rank = jnp.concatenate(ranks, axis=1)
+    return jnp.sum(jnp.where(member, rank, 0.0), axis=0, keepdims=True)
+
+
+def column_of(row):
+    diagonal = iota((LANES, LANES), 0) == iota((LANES, LANES), 1)
+    pieces = []
+    for begin in range(0, row.shape[1], LANES):
+        piece = jnp.where(diagonal, row[:, begin : begin + LANES], 0.0)
+        pieces.append(jnp.sum(piece, axis=1, keepdims=True))
+    return jnp.concatenate(pieces, axis=0)
+
+
+def last_row(ref, block, size):
+    begin = block * size + size - 8
+    return ref[begin : begin + 8, :].astype(jnp.float32)[7:8, :]
+
+
+def pack_kernel(members, group_codes, owner_ref, offset_ref, first_ref, second_ref, x_ref, send_ref, slot_ref):
+    rows, feat = x_ref.shape
+    group = owner_ref[...] // members
+    relay = (group * group_codes + offset_ref[...]) % members
+    rank = rank_in_bin(iota((members, rows), 0) == relay).astype(jnp.int32)
+    fits = rank < BLOCK_RELAY - 1
+    full = jnp.max(jnp.where(fits, 0.0, 1.0))
+    slot_ref[...] = jnp.where(fits, relay * BLOCK_RELAY + rank, -1)
+    rank = jnp.where(fits, rank, -1)
+    kind = iota((16, rows), 0)
+    labels = jnp.where(kind == FIRST, first_ref[...] + 1, 0)
+    labels = jnp.where(kind == SECOND, second_ref[...], labels)
+    labels = jnp.where(kind == GROUP, group, labels)
+    labels = labels.astype(jnp.float32).astype(jnp.bfloat16)
+    x = x_ref[...]
+    full_row = jnp.full((1, feat - 3 * LANES), full, jnp.float32)
+    is_last = iota((BLOCK_RELAY, feat), 0) == BLOCK_RELAY - 1
+    for block in range(members):
+        begin = block * BLOCK_RELAY
+        chosen = hot((iota((LANES, rows), 0) == rank) & (relay == block))
+        kinds = dot_nt(labels, chosen)
+        last = [kinds[kind : kind + 1] for kind in (FIRST, SECOND, GROUP)] + [full_row]
+        last = jnp.concatenate(last, axis=1)
+        moved = dot(chosen[:BLOCK_RELAY], x)
+        send_ref[begin : begin + BLOCK_RELAY, :] = jnp.where(is_last, last, moved).astype(jnp.bfloat16)
+
+
+def relay_kernel(got_ref, send_ref, place_ref):
+    total, feat = got_ref.shape
+    sources = total // BLOCK_RELAY
+    groups = send_ref.shape[0] // BLOCK_CODE
+    labels = []
+    full = jnp.zeros((1, 1), jnp.float32)
+    for block in range(sources):
+        row = last_row(got_ref, block, BLOCK_RELAY)
+        full = jnp.maximum(full, row[:, 3 * LANES : 3 * LANES + 1])
+        kinds = [row[:, kind * LANES : kind * LANES + BLOCK_RELAY] for kind in (FIRST, SECOND, GROUP)]
+        kinds.append(jnp.zeros((13, BLOCK_RELAY), jnp.float32))
+        labels.append(jnp.concatenate(kinds, axis=0))
+    labels = jnp.concatenate(labels, axis=1)
+    live = labels[FIRST : FIRST + 1] > 0.5
+    group = labels[GROUP : GROUP + 1]
+    member = (iota((16, total), 0).astype(jnp.float32) == group) & live
+    rank = rank_in_bin(member)
+    fits = rank < BLOCK_CODE - 1
+    full = jnp.maximum(full, jnp.max(jnp.where(live & ~fits, 1.0, 0.0)))
+    place = jnp.where(live & fits, group * BLOCK_CODE + rank, -1.0)
+    place_ref[...] = column_of(place).astype(jnp.int32)
+    place = place.astype(jnp.int32)
+    labels = labels.astype(jnp.bfloat16)
+    got = got_ref[...]
+    empty = jnp.zeros((1, 2 * LANES - BLOCK_CODE), jnp.float32)
+    full_row = jnp.broadcast_to(full, (1, feat - 4 * LANES))
+    is_last = iota((BLOCK_CODE, feat), 0) == BLOCK_CODE - 1
+    for block in range(groups):
+        begin = block * BLOCK_CODE
+        chosen = hot(iota((BLOCK_CODE, total), 0) + begin == place)
+        kinds = dot_nt(labels, chosen)
+        last = [kinds[FIRST : FIRST + 1], empty, kinds[SECOND : SECOND + 1], empty, full_row]
+        last = jnp.concatenate(last, axis=1)
+        send_ref[begin : begin + BLOCK_CODE, :] = jnp.where(is_last, last, dot(chosen, got)).astype(
+            jnp.bfloat16
+        )
+
+
+def code_kernel(got_ref, start_ref, out_ref, mine, start, sem):
+    total, feat = got_ref.shape
+    group_codes, codes_two = start_ref.shape[:2]
+    sources = total // BLOCK_CODE
+    offset = (lax.axis_index("mem") + 16 * group_codes - group_codes * lax.axis_index("grp")) % 16
+    fetch = pltpu.make_async_copy(start_ref.at[jnp.minimum(offset, group_codes - 1)], mine, sem)
+    fetch.start()
+    labels = []
+    full = jnp.zeros((1, 1), jnp.float32)
+    for block in range(sources):
+        row = last_row(got_ref, block, BLOCK_CODE)
+        full = jnp.maximum(full, row[:, 4 * LANES : 4 * LANES + 1])
+        kinds = [row[:, 2 * kind * LANES : 2 * kind * LANES + BLOCK_CODE] for kind in (FIRST, SECOND)]
+        kinds.append(jnp.zeros((6, BLOCK_CODE), jnp.float32))
+        labels.append(jnp.concatenate(kinds, axis=0))
+    labels = jnp.concatenate(labels, axis=1)
+    first = labels[FIRST : FIRST + 1] - 1.0
+    second = jnp.where(first >= 0.0, labels[SECOND : SECOND + 1], -1.0)
+    x = got_ref[...]
+    cluster = iota((LANES, total), 0).astype(jnp.float32)
+    fetch.wait()
+    start[...] = jnp.zeros_like(start)
+    start[0:codes_two, :] = mine[...].astype(jnp.float32)
+
+    def update(earlier, assigned):
+        member = hot(cluster == assigned)
+        totals = dot(member, x)
+        counts = jnp.sum(member.astype(jnp.float32), axis=1, keepdims=True)
+        return (totals + PRIOR * earlier) / (counts + PRIOR)
+
+    diagonal = iota((LANES, LANES), 0) == iota((LANES, LANES), 1)
+
+    def squares_of(rounded):
+        wide = rounded.astype(jnp.float32)
+        down = jnp.sum(wide * wide, axis=1, keepdims=True)
+        return jnp.sum(jnp.where(diagonal, down, 0.0), axis=0, keepdims=True)
+
+    centre_one = update(start[...], first)
+    rounded_one = centre_one.astype(jnp.bfloat16)
+    centre_two = update(centre_one, second)
+    rounded_two = centre_two.astype(jnp.bfloat16)
+    squares_one = squares_of(rounded_one)
+    squares_two = squares_of(rounded_two)
+    wide_x = x.astype(jnp.float32)
+    squares = jnp.sum(wide_x * wide_x, axis=1, keepdims=True)
+    lane = iota((total, LANES), 1)
+    near = (squares - 2.0 * dot_nt(x, rounded_one) + squares_one) / feat
+    near = jnp.where(lane.astype(jnp.float32) == column_of(first), near, 0.0)
+    near = jnp.sum(near, axis=1, keepdims=True)
+    score = (squares - 2.0 * dot_nt(x, rounded_two) + squares_two) / feat
+    score = jnp.where(lane == codes_two, near, score)
+    out_ref[...] = jnp.where(lane > codes_two, full, score)
+
+
+def unrelay_kernel(got_ref, place_ref, out_ref):
+    total = got_ref.shape[0]
+    got = got_ref[...]
+    full = jnp.max(got[:, LANES - 1 :])
+    terms = jnp.concatenate(three_terms(got), axis=1)
+    for begin in range(0, out_ref.shape[0], LANES):
+        chosen = hot(iota((LANES, total), 1) == place_ref[begin : begin + LANES, :])
+        moved = dot(chosen, terms)
+        moved = moved[:, :LANES] + (moved[:, LANES : 2 * LANES] + moved[:, 2 * LANES :])
+        out_ref[begin : begin + LANES, :] = jnp.where(iota((LANES, LANES), 1) == LANES - 1, full, moved)
+
+
+def unpack_kernel(got_ref, slot_ref, all_ref, one_ref, full_ref):
+    total = got_ref.shape[0]
+    rows = slot_ref.shape[1]
+    codes_two = all_ref.shape[0]
+    got = got_ref[...]
+    full_ref[0, 0] = (jnp.max(got[:, LANES - 1 :]) > 0.5).astype(jnp.int32)
+    high, middle, low = three_terms(got.T)
+    chosen = hot(iota((total, rows), 0) == slot_ref[...])
+    moved = dot(high, chosen) + (dot(middle, chosen) + dot(low, chosen))
+    all_ref[...] = moved[:codes_two]
+    one_ref[...] = moved[codes_two : codes_two + 1]
+
+
+def over_members(totals, counts):
+    members = lax.axis_size("mem")
+    clusters, feat = totals.shape
+    share = -(-clusters // members)
+
+    def swap(blocks):
+        return lax.all_to_all(blocks, "mem", split_axis=0, concat_axis=0, tiled=True)
+
+    padded = jnp.pad(totals.astype(jnp.bfloat16), ((0, members * share - clusters), (0, 0)))
+    own = jnp.sum(swap(padded.reshape(members, share, feat)).astype(jnp.float32), axis=0)
+    own = jnp.broadcast_to(own.astype(jnp.bfloat16)[None], (members, share, feat))
+    summed = swap(own).reshape(members * share, feat)[:clusters].astype(jnp.float32)
+    counted = jnp.sum(swap(jnp.broadcast_to(counts[None], (members, clusters))), axis=0)
+    return summed, counted
 
 
 def pick_block(total):
@@ -13,7 +244,7 @@
     return total
 
 
-def body(embeddings, initial_centroids, row_owner, prefix_offset, first_assign, second_assign):
+def general(embeddings, initial_centroids, row_owner, prefix_offset, first_assign, second_assign):
     row_count, feat_width = embeddings.shape
     group_codes = initial_centroids.shape[0]
     codes_two = initial_centroids.shape[1]
@@ -71,10 +302,7 @@
 
     def update(earlier, cluster_ids):
         totals, counts = local_totals(cluster_ids)
-        totals, counts = (
-            lax.psum(totals.astype(jnp.bfloat16), "mem").astype(jnp.float32),
-            lax.psum(counts.astype(jnp.bfloat16), "mem").astype(jnp.float32),
-        )
+        totals, counts = over_members(totals, counts)
         centre = (totals + PRIOR * earlier) / (counts[:, None] + PRIOR)
         return (centre, centre.astype(jnp.bfloat16))
 
@@ -121,6 +349,71 @@
     return (distances, first_distance)
 
 
+def quick(embeddings, initial_centroids, row_owner, prefix_offset, first_assign, second_assign):
+    rows, feat = embeddings.shape
+    group_codes, codes_two = initial_centroids.shape[:2]
+    groups = lax.axis_size("grp")
+    members = lax.axis_size("mem")
+    relay_total = members * BLOCK_RELAY
+    code_total = groups * BLOCK_CODE
+    shape = jax.ShapeDtypeStruct
+    vmem = pl.BlockSpec(memory_space=pltpu.VMEM)
+
+    def swap(array, axis, count):
+        blocks = array.reshape(count, array.shape[0] // count, array.shape[1])
+        return lax.all_to_all(blocks, axis, split_axis=0, concat_axis=0, tiled=True).reshape(array.shape)
+
+    send, slot = call(
+        lambda *refs: pack_kernel(members, group_codes, *refs),
+        [shape((relay_total, feat), jnp.bfloat16), shape((1, rows), jnp.int32)],
+        [
+            row_owner.reshape(1, rows),
+            prefix_offset.reshape(1, rows),
+            first_assign.reshape(1, rows),
+            second_assign.reshape(1, rows),
+            embeddings,
+        ],
+    )
+    got = swap(send, "mem", members)
+    send, place = call(
+        relay_kernel,
+        [shape((code_total, feat), jnp.bfloat16), shape((relay_total, 1), jnp.int32)],
+        [got],
+    )
+    got = swap(send, "grp", groups)
+    (scored,) = call(
+        code_kernel,
+        [shape((code_total, LANES), jnp.float32)],
+        [got, initial_centroids],
+        in_memory=[vmem, pl.BlockSpec(memory_space=pl.ANY)],
+        scratch=[
+            pltpu.VMEM((codes_two, feat), jnp.bfloat16),
+            pltpu.VMEM((LANES, feat), jnp.float32),
+            pltpu.SemaphoreType.DMA,
+        ],
+    )
+    back = swap(scored, "grp", groups)
+    (back,) = call(unrelay_kernel, [shape((relay_total, LANES), jnp.float32)], [back, place])
+    back = swap(back, "mem", members)
+    return call(
+        unpack_kernel,
+        [shape((codes_two, rows), jnp.float32), shape((1, rows), jnp.float32), shape((1, 1), jnp.int32)],
+        [back, slot],
+        out_memory=[vmem, vmem, pl.BlockSpec(memory_space=pltpu.SMEM)],
+    )
+
+
+def body(*inputs):
+    distances, first_distance, full = quick(*inputs)
+    return lax.cond(
+        full[0, 0] > 0,
+        lambda kept, given: general(*given),
+        lambda kept, given: kept,
+        (distances, first_distance[0]),
+        inputs,
+    )
+
+
 def solution(mesh):
     placed = (
         P(("grp", "mem"), None),

time: 317 us -> 110 us (0.35)
  waiting for transfers between devices: 117 us -> 11.1 us
  local copies, waits for them, and re-layouts: 50.9 us -> 0.7 us
  blocking collectives: 32.6 us -> 77.8 us
  other arithmetic: 34.4 us -> 0 us
  matrix products: 32.4 us -> 0 us
  starting transfers between devices: 34.2 us -> 3.58 us
  Pallas kernels: 0 us -> 14 us
  between operations: 14.4 us -> 1.41 us
    all_to_all x0 -> x3, blocking collectives: none -> 77.8 us  [swap(): lax.all_to_all(blocks, axis, split_axis=0, concat_axis=0, tiled=True)]
    psum x1 -> x0, waiting for transfers between devices: 60.2 us -> none  [update(): lax.psum(totals.astype(jnp.bfloat16), 'mem').astype(jnp.float32)]
    all_to_all x4 -> x1, waiting for transfers between devices: 56.8 us -> 11.1 us  [swap(): lax.all_to_all(blocks, axis, split_axis=0, concat_axis=0, tiled=True)]
    psum x1 -> x0, blocking collectives: 32.6 us -> none  [update(): lax.psum(counts.astype(jnp.bfloat16), 'mem').astype(jnp.float32)]
    dot_general x6 -> x0, matrix products: 32.4 us -> none  [the longest x4 21.2 us: add_block(): lax.dot_general(hot_table, block_x, (((0,), (0,)), ((), ())), preferred_e...]
    all_to_all x4 -> x1, starting transfers between devices: 34 us -> 3.58 us  [swap(): lax.all_to_all(blocks, axis, split_axis=0, concat_axis=0, tiled=True)]
    reduce_sum x10 -> x0, other arithmetic: 20.5 us -> none  [the longest x2 5.9 us: score_block(): inner = jnp.sum(raw * select[:, None, :], axis=0)]
    gather x4 -> x0, local copies, waits for them, and re-layouts: 14.8 us -> none  [the longest x2 10.6 us: body(): jnp.take(rounded_one, jnp.maximum(ids_one, 0), axis=0).astype(jnp.float32)]
  transfers between devices with their start and end apart: 5 -> 1, of which waited for: 4 -> 1; matrix products, arithmetic and copies ran while one was open for 15% -> 0% of each run, Pallas kernels for 0% -> 0%
where the time goes in v2:
time: 110 us; the launch traced here: 109 us
  blocking collectives  77.8 us (71%)
  Pallas kernels  14 us (13%)
  waiting for transfers between devices  11.1 us (10%)
  starting transfers between devices  3.58 us (3%)
  between operations  1.41 us (1%)
    all_to_all x3, blocking collectives, swap(): lax.all_to_all(blocks, axis, split_axis=0, concat_axis=0, tiled=True)  77.8 us
    pallas_call x5, Pallas kernels, call(): pl.pallas_call(kernel, out_shape=out_shape, in_specs=in_memory or [vmem]...  14 us
    all_to_all x1, waiting for transfers between devices, swap(): lax.all_to_all(blocks, axis, split_axis=0, concat_axis=0, tiled=True)  11.1 us
    all_to_all x1, starting transfers between devices, swap(): lax.all_to_all(blocks, axis, split_axis=0, concat_axis=0, tiled=True)  3.58 us
  transfers between devices with their start and end apart: 1, of which 1 were waited for; matrix products, arithmetic and copies ran while one was open for 0% of the time, Pallas kernels for 0%

profile of v2, /device:TPU:1, one launch (start us, length us, event | category | flops | bytes accessed | tf_op | source)
XLA Modules:
  0.0 108.9 jit_solution(13407987012685986440)
XLA Ops:
  0.6 4.0 %shard_map.79 = (bf16[1152,768]{1,0:T(8,128)(2,1)S(1)}, s32[1,512]{1,0:T(1,128)S(1)}) custom-call(s32[1,512]{1,0:T(1,128)} %bitcast.100, s32[1,512]{1,0:T(1,128)} %bitcast.104, s32[1,512]{1,0:T(1,128)} %bitcast.106, s32[1,512]{1,0:T(1,128)} %bitcast.108, bf16[512,768]{1,0:T(8,128)(2,1)} %refs_4_.1), custom_call_target="tpu_custom_call" | custom-call | tf_op jit(solution)/shard_map/pallas_call | solution.py:43
  4.7 32.4 %all_to_all.76 = bf16[16,72,768]{2,1,0:T(8,128)(2,1)S(1)} all-to-all(bf16[16,72,768]{2,1,0:T(8,128)(2,1)S(1)} %bitcast.96), channel_id=1, replica_groups=mesh['grp'=8,'mem'=16] {'mem'}, dimensions={0} | all-to-all | bytes 3538944 | tf_op jit(solution)/shard_map/all_to_all | solution.py:364
  37.1 0.0 copy-start.2
  37.1 3.8 %shard_map.80 = (bf16[1280,768]{1,0:T(8,128)(2,1)S(1)}, s32[1152,1]{1,0:T(8,128)S(1)}) custom-call(bf16[1152,768]{1,0:T(8,128)(2,1)S(1)} %bitcast.91), custom_call_target="tpu_custom_call" | custom-call | tf_op jit(solution)/shard_map/pallas_call | solution.py:43
  40.8 31.1 %all_to_all.77 = bf16[8,160,768]{2,1,0:T(8,128)(2,1)S(1)} all-to-all(bf16[8,160,768]{2,1,0:T(8,128)(2,1)S(1)} %bitcast.95), channel_id=1, replica_groups=mesh['grp'=8,'mem'=16] {'grp'}, dimensions={0} | all-to-all | bytes 3932160 | tf_op jit(solution)/shard_map/all_to_all | solution.py:364
  72.0 0.0 copy-done.2
  72.0 2.3 %shard_map.81 = f32[1280,128]{1,0:T(8,128)S(1)} custom-call(bf16[1280,768]{1,0:T(8,128)(2,1)S(1)} %bitcast.90, bf16[13,100,768]{2,1,0:T(8,128)(2,1)S(1)} %copy-done.2), custom_call_target="tpu_custom_call" | custom-call | tf_op jit(solution)/shard_map/pallas_call | solution.py:43
  74.3 0.0 copy-start.5
  74.3 0.0 copy-start.7
  74.3 0.0 copy-start.8
  74.3 0.0 copy-start.9
  74.4 14.3 %all_to_all.78 = f32[8,160,128]{2,1,0:T(8,128)S(1)} all-to-all(f32[8,160,128]{2,1,0:T(8,128)S(1)} %bitcast.93), channel_id=1, replica_groups=mesh['grp'=8,'mem'=16] {'grp'}, dimensions={0} | all-to-all | bytes 1310720 | tf_op jit(solution)/shard_map/all_to_all | solution.py:364
  88.7 2.6 %shard_map.82 = f32[1152,128]{1,0:T(8,128)} custom-call(f32[1280,128]{1,0:T(8,128)S(1)} %bitcast.92, s32[1152,1]{1,0:T(8,128)S(1)} %get-tuple-element.146.place_ref), custom_call_target="tpu_custom_call" | custom-call | tf_op jit(solution)/shard_map/pallas_call | solution.py:43
  91.3 3.6 %all-to-all-start.13 = ((f32[16,72,128]{2,1,0:T(8,128)}), f32[16,72,128]{2,1,0:T(8,128)S(1)}, u32[]{:S(2)}, u32[]{:S(2)}) async-start(f32[16,72,128]{2,1,0:T(8,128)} %bitcast.25), calls=%async_computation.13 | async-start | bytes 1179648 | tf_op jit(solution)/shard_map/all_to_all | solution.py:364
  94.9 11.1 %all-to-all-done.13 = f32[16,72,128]{2,1,0:T(8,128)S(1)} async-done(((f32[16,72,128]{2,1,0:T(8,128)}), f32[16,72,128]{2,1,0:T(8,128)S(1)}, u32[]{:S(2)}, u32[]{:S(2)}) %all-to-all-start.13) | async-done | bytes 589856 | tf_op jit(solution)/shard_map/all_to_all | solution.py:364
  106.0 1.3 %shard_map.83 = (f32[100,512]{1,0:T(8,128)S(1)}, f32[1,512]{1,0:T(1,128)S(1)}, s32[1,1]{1,0:T(1,128)}) custom-call(f32[1152,128]{1,0:T(8,128)S(1)} %bitcast.94, s32[1,512]{1,0:T(1,128)S(1)} %get-tuple-element.147.slot_ref), custom_call_target="tpu_custom_call" | custom-call | tf_op jit(solution)/shard_map/pallas_call | solution.py:43
  107.9 0.0 copy-done.5
  107.9 0.0 copy-done.7
  108.0 0.0 copy-done.8
  108.0 0.0 copy-done.9
  108.0 0.2 conditional.1
  108.2 0.0 copy-start.10
  108.2 0.0 copy-start.11
  108.2 0.7 copy-done.10
  108.9 0.0 copy-done.11
Async XLA Ops:
  37.1 34.9 %copy-start.2 = (bf16[13,100,768]{2,1,0:T(8,128)(2,1)S(1)}, bf16[13,100,768]{2,1,0:T(8,128)(2,1)}, u32[]{:S(2)}) copy-start(bf16[13,100,768]{2,1,0:T(8,128)(2,1)} %start_ref.1) | copy-start | bytes 5990404
  74.3 33.6 %copy-start.5 = (s32[512,1]{0,1:T(1,128)S(1)}, s32[512,1]{0,1:T(1,128)}, u32[]{:S(2)}) copy-start(s32[512,1]{0,1:T(1,128)} %param.16) | copy-start | bytes 6148
  74.3 33.6 %copy-start.7 = (s32[512]{0:T(512)S(1)}, s32[512]{0:T(512)}, u32[]{:S(2)}) copy-start(s32[512]{0:T(512)} %param.17) | copy-start | bytes 6148
  74.3 33.6 %copy-start.8 = (s32[512]{0:T(512)S(1)}, s32[512]{0:T(512)}, u32[]{:S(2)}) copy-start(s32[512]{0:T(512)} %param.18) | copy-start | bytes 6148
  74.3 33.6 %copy-start.9 = (s32[512]{0:T(512)S(1)}, s32[512]{0:T(512)}, u32[]{:S(2)}) copy-start(s32[512]{0:T(512)} %param.19) | copy-start | bytes 6148
  91.3 14.7 %all-to-all-start.13 = ((f32[16,72,128]{2,1,0:T(8,128)}), f32[16,72,128]{2,1,0:T(8,128)S(1)}, u32[]{:S(2)}, u32[]{:S(2)}) async-start(f32[16,72,128]{2,1,0:T(8,128)} %bitcast.25), calls=%async_computation.13 | async-start | bytes 1179648 | tf_op jit(solution)/shard_map/all_to_all | solution.py:364
  108.2 0.7 copy-start.10
  108.2 0.7 copy-start.11
